TPU v7x, 32 devices: a whole 2x2x4 slice. The times are simulated.
32 devices in a mesh: blk: 16 (over z, y, x), scale: 2 (over core).
Axes of the slice: x: 2, y: 2, z: 4, core: 2. Of those that a mesh axis runs over, the one named last changes fastest.
Arguments:
- start_block: float32 [64, 32768], P(None, ('blk', 'scale')), may hold values from -90 to 90
- blocks: bfloat16 [1024, 128, 128], P(('blk', 'scale')), may hold values from -0.1875 to 0.1875
- block_column: int32 [1024], P(('blk', 'scale')), may hold values from 0 to 7
- block_target: int32 [1024], P(('blk', 'scale')), may hold values from 0 to 15, as said below
- block_count: int32 [32], P(('blk', 'scale')), may hold values from 2 to 32, as said below
- partner: int32 [32768], P(('blk', 'scale')), may hold values from 0 to 1023, as said below
- degree: int32 [32768], P(('blk', 'scale')), may hold values from 1 to 16
Outputs:
- subspace: float32 [64, 32768], P(None, ('blk', 'scale'))
- rayleigh: float32 [64, 64], replicated
Inputs may be any that keep to these rules, and one draw needn't show every extreme that they name: block_count[g] is the number of live slots of row group g; it is at least 2; some row group has all 32 slots live in every draw. In each row group, slots c < 2 have block_target of 8 or more, and all other slots have block_target below 8. Within each row group, partner is a permutation of 0 to 1023, and the pairing is mutual: if node i of group (b, s) has partner j, then node j of group (b, s xor 1) has partner i.
All inputs are finite; a program needn't handle non-finite values.
Results may differ from a plain program's by a relative error of at most 0.0011.
Values may be sent and summed in bfloat16 or wider, within the bound.
A program may use at most 64 MiB of HBM per device.

v0:
```python
import jax
import jax.numpy as jnp
from jax import lax
from jax.sharding import PartitionSpec as P

ITERS = 2


FULL_PRECISION = lax.Precision.HIGHEST


def from_behind(block, axis, distance):
    devices = range(lax.axis_size(axis))
    route = [((i - distance) % len(devices), i) for i in devices]
    return lax.ppermute(block, axis, route)


def swapped(array, axis, apart):
    return lax.ppermute(array, axis, [(i, i ^ 1 << apart) for i in range(lax.axis_size(axis))])


def pick_rows(onehot, source):
    picked = jnp.einsum(
        "cr,krj->ckj", onehot.astype(jnp.bfloat16), source, preferred_element_type=jnp.float32
    )
    return picked.astype(jnp.bfloat16)


def place_rows(onehot, partial_terms):
    return jnp.einsum("cr,ckj->krj", onehot, partial_terms, precision=FULL_PRECISION)


def slot_masks(columns, targets, slot_count, row_blocks):
    live_mask = (jnp.arange(columns.shape[0]) < slot_count[0]).astype(jnp.float32)[:, None]
    onecol = (columns[:, None] == jnp.arange(row_blocks)[None, :]).astype(jnp.float32) * live_mask
    onetgt = (targets[:, None] == jnp.arange(2 * row_blocks)[None, :]).astype(
        jnp.float32
    ) * live_mask
    return (onecol, onetgt)


def forward_terms(source, weights, onecol):
    picked = pick_rows(onecol, source)
    return jnp.einsum("cki,cji->ckj", picked, weights, preferred_element_type=jnp.float32)


def backward_terms(stacked, weights, onetgt):
    picked = pick_rows(onetgt, stacked)
    return jnp.einsum("ckj,cji->cki", picked, weights, preferred_element_type=jnp.float32)


def over_slots(term_fn, slot_total, initial):
    return jax.tree.map(jnp.add, initial, term_fn(0, slot_total))


def apply_operator(
    vectors, inv_sqrt_degree, blocks, block_column, block_target, block_count, partner
):
    vector_count, node_rows = vectors.shape
    row_blocks = node_rows // 128
    scaled = (vectors * inv_sqrt_degree[None, :]).astype(jnp.bfloat16)
    own_vectors = scaled.reshape(vector_count, row_blocks, 128)
    next_vectors = from_behind(own_vectors, "blk", -1)
    stacked = jnp.concatenate([own_vectors, next_vectors], axis=1)
    onecol, onetgt = slot_masks(block_column, block_target, block_count, row_blocks)
    empty_sum = jnp.zeros((vector_count, row_blocks, 128), jnp.float32)

    def local_terms(first_slot, slot_width):
        forward = forward_terms(own_vectors, blocks, onecol)
        backward = backward_terms(stacked, blocks, onetgt)
        nearby = place_rows(onetgt[:, :row_blocks], forward) + place_rows(onecol, backward)
        return (nearby, place_rows(onetgt[:, row_blocks:], forward))

    nearby, ahead_sum = over_slots(local_terms, blocks.shape[0], (empty_sum, empty_sum))
    surface = nearby + from_behind(ahead_sum.astype(jnp.bfloat16), "blk", 1).astype(ahead_sum.dtype)
    partner_vectors = swapped(scaled, "scale", 0)
    crossed = jnp.take(partner_vectors, partner, axis=1).astype(jnp.float32)
    return vectors + inv_sqrt_degree[None, :] * (surface.reshape(vector_count, node_rows) + crossed)


def shards(start_block, blocks, block_column, block_target, block_count, partner, degree):
    inv_sqrt_degree = 1.0 / jnp.sqrt(degree.astype(jnp.float32))
    vector_count = start_block.shape[0]
    node_total = start_block.shape[1] * lax.axis_size("blk") * lax.axis_size("scale")

    def operate(vectors):
        return apply_operator(
            vectors, inv_sqrt_degree, blocks, block_column, block_target, block_count, partner
        )

    subspace = start_block
    for sweep_index in range(ITERS):
        orthonormal_images = operate(subspace)
        local_gram = jnp.dot(orthonormal_images, orthonormal_images.T, precision=FULL_PRECISION)
        gram_matrix = lax.psum(local_gram, ("blk", "scale")) / node_total
        factor = jnp.linalg.cholesky(gram_matrix)
        factor_inverse = jax.scipy.linalg.solve_triangular(
            factor, jnp.eye(vector_count, dtype=jnp.float32), lower=True
        )
        subspace = jnp.dot(factor_inverse, orthonormal_images, precision=FULL_PRECISION)
    images = operate(subspace)
    local_projection = jnp.dot(subspace, images.T, precision=FULL_PRECISION)
    rayleigh = lax.psum(local_projection, ("blk", "scale")) / node_total
    return (subspace, rayleigh)


def solution(mesh):
    return jax.shard_map(
        shards,
        mesh=mesh,
        in_specs=(
            P(None, ("blk", "scale")),
            P(("blk", "scale"), None, None),
            P(("blk", "scale")),
            P(("blk", "scale")),
            P(("blk", "scale")),
            P(("blk", "scale")),
            P(("blk", "scale")),
        ),
        out_specs=(P(None, ("blk", "scale")), P()),
        check_vma=False,
    )
```

profile of v0, /device:TPU:0, one launch (start us, length us, event | category | flops | bytes accessed | tf_op | source)
XLA Modules:
  0.0 202.4 jit_solution(17537485149810660932)
XLA Ops:
  0.6 0.8 convert_rsqrt_fusion
  1.4 1.0 fusion.136
  2.4 7.0 %collective-permute-start = (bf16[64,8,128]{2,1,0:T(8,128)(2,1)S(1)}, bf16[64,8,128]{2,1,0:T(8,128)(2,1)S(1)}, u32[]{:S(2)}, u32[]{:S(2)}) collective-permute-start(bf16[64,8,128]{2,1,0:T(8,128)(2,1)S(1)} %bitcast.141), channel_id=1, source_target_pairs={{2,0},{4,2},{6,4},{8,6},{10,8},{12,10},{14,12},{16,14},{18,16},{20... | collective-permute-start | bytes 393224 | tf_op jit(solution)/shard_map/ppermute | solution.py:15
  11.4 0.8 fusion.18
  12.2 1.2 fusion.3
  13.7 1.2 fusion.16
  16.4 3.2 %gather_fusion = bf16[1024,64]{1,0:T(8,128)(2,1)S(1)} fusion(bf16[64,1024]{0,1:T(8,128)(2,1)S(1)} %copy.11, s32[1024]{0:T(1024)S(1)} %fusion.73), kind=kCustom, calls=%fused_computation.clone | custom fusion | bytes 266240 | tf_op jit(solution)/shard_map/jit(_take)/gather | solution.py:77
  19.8 2.3 %collective-permute-done.1 = bf16[64,8,128]{2,1,0:T(8,128)(2,1)S(1)} collective-permute-done((bf16[64,8,128]{2,1,0:T(8,128)(2,1)S(1)}, bf16[64,8,128]{2,1,0:T(8,128)(2,1)S(1)}, u32[]{:S(2)}, u32[]{:S(2)}) %collective-permute-start.1) | collective-permute-done | bytes 131104 | tf_op jit(solution)/shard_map/ppermute | solution.py:15
  22.1 1.9 convert_add_fusion.2
  24.0 0.7 copy-done.7
  25.1 37.9 %psum.21 = f32[64,64]{0,1:T(8,128)S(1)} all-reduce(f32[64,64]{0,1:T(8,128)S(1)} %fusion.118), channel_id=1, replica_groups=mesh['blk'=16,'scale'=2] {'blk','scale'}, use_global_device_ids=true, to_apply=%region_0.0 | all-reduce | flops 4096 | bytes 32768 | tf_op jit(solution)/shard_map/psum | solution.py:95
  63.1 5.8 %cholesky.44 = f32[64,64]{1,0:T(8,128)S(1)} custom-call(f32[64,64]{1,0:T(8,128)S(1)} %fusion.60), custom_call_target="Cholesky" | custom-call | tf_op jit(solution)/shard_map/jit(cholesky)/cholesky | solution.py:96
  70.3 4.9 %custom-call.6 = f32[1,64,64]{1,2,0:T(8,128)S(1)} custom-call(f32[1,64,64]{2,1,0:T(8,128)S(1)} %fusion.55), custom_call_target="InvertDiagBlocksLowerTriangular" | custom-call | tf_op jit(solution)/shard_map/jit(_solve_triangular)/triangular_solve | solution.py:97
  76.9 3.2 %collective-permute-start.3 = (bf16[64,8,128]{2,1,0:T(8,128)(2,1)S(1)}, bf16[64,8,128]{2,1,0:T(8,128)(2,1)S(1)}, u32[]{:S(2)}, u32[]{:S(2)}) collective-permute-start(bf16[64,8,128]{2,1,0:T(8,128)(2,1)S(1)} %bitcast.148), channel_id=1, source_target_pairs={{2,0},{4,2},{6,4},{8,6},{10,8},{12,10},{14,12},{16,14},{18,16},{20... | collective-permute-start | bytes 393224 | tf_op jit(solution)/shard_map/ppermute | solution.py:15
  80.2 0.8 fusion.20
  81.0 1.2 fusion.4
  82.5 1.2 fusion.13
  84.7 3.2 %gather_fusion.1 = bf16[1024,64]{1,0:T(8,128)(2,1)S(1)} fusion(bf16[64,1024]{0,1:T(8,128)(2,1)S(1)} %copy.17, s32[1024]{0:T(1024)S(1)} %fusion.73), kind=kCustom, calls=%fused_computation.1.clone | custom fusion | bytes 266240 | tf_op jit(solution)/shard_map/jit(_take)/gather | solution.py:77
  88.0 4.0 %collective-permute-done.4 = bf16[64,8,128]{2,1,0:T(8,128)(2,1)S(1)} collective-permute-done((bf16[64,8,128]{2,1,0:T(8,128)(2,1)S(1)}, bf16[64,8,128]{2,1,0:T(8,128)(2,1)S(1)}, u32[]{:S(2)}, u32[]{:S(2)}) %collective-permute-start.4) | collective-permute-done | bytes 131104 | tf_op jit(solution)/shard_map/ppermute | solution.py:15
  92.0 1.9 convert_add_fusion.1
  95.0 37.4 %psum.22 = f32[64,64]{0,1:T(8,128)S(1)} all-reduce(f32[64,64]{0,1:T(8,128)S(1)} %fusion.122), channel_id=1, replica_groups=mesh['blk'=16,'scale'=2] {'blk','scale'}, use_global_device_ids=true, to_apply=%region_3.7 | all-reduce | flops 4096 | bytes 32768 | tf_op jit(solution)/shard_map/psum | solution.py:95
  132.5 5.8 %cholesky.55 = f32[64,64]{1,0:T(8,128)S(1)} custom-call(f32[64,64]{1,0:T(8,128)S(1)} %fusion.58), custom_call_target="Cholesky" | custom-call | tf_op jit(solution)/shard_map/jit(cholesky)/cholesky | solution.py:96
  139.7 4.9 %custom-call.7 = f32[1,64,64]{1,2,0:T(8,128)S(1)} custom-call(f32[1,64,64]{2,1,0:T(8,128)S(1)} %fusion.56), custom_call_target="InvertDiagBlocksLowerTriangular" | custom-call | tf_op jit(solution)/shard_map/jit(_solve_triangular)/triangular_solve | solution.py:97
  146.4 4.1 %collective-permute-start.6 = (bf16[64,8,128]{2,1,0:T(8,128)(2,1)S(1)}, bf16[64,8,128]{2,1,0:T(8,128)(2,1)S(1)}, u32[]{:S(2)}, u32[]{:S(2)}) collective-permute-start(bf16[64,8,128]{2,1,0:T(8,128)(2,1)S(1)} %bitcast.145), channel_id=1, source_target_pairs={{2,0},{4,2},{6,4},{8,6},{10,8},{12,10},{14,12},{16,14},{18,16},{20... | collective-permute-start | bytes 393224 | tf_op jit(solution)/shard_map/ppermute | solution.py:15
  150.5 0.8 fusion.22
  151.3 1.3 fusion.5
  152.9 1.2 fusion.10
  155.0 3.2 %gather_fusion.2 = bf16[1024,64]{1,0:T(8,128)(2,1)S(1)} fusion(bf16[64,1024]{0,1:T(8,128)(2,1)S(1)} %copy.23, s32[1024]{0:T(1024)S(1)} %fusion.73), kind=kCustom, calls=%fused_computation.2.clone | custom fusion | bytes 266240 | tf_op jit(solution)/shard_map/jit(_take)/gather | solution.py:77
  158.4 3.9 %collective-permute-done.7 = bf16[64,8,128]{2,1,0:T(8,128)(2,1)S(1)} collective-permute-done((bf16[64,8,128]{2,1,0:T(8,128)(2,1)S(1)}, bf16[64,8,128]{2,1,0:T(8,128)(2,1)S(1)}, u32[]{:S(2)}, u32[]{:S(2)}) %collective-permute-start.7) | collective-permute-done | bytes 131104 | tf_op jit(solution)/shard_map/ppermute | solution.py:15
  162.4 1.2 convert_add_fusion
  164.7 37.0 %psum.23 = f32[64,64]{0,1:T(8,128)S(1)} all-reduce(f32[64,64]{0,1:T(8,128)S(1)} %fusion.24), channel_id=1, replica_groups=mesh['blk'=16,'scale'=2] {'blk','scale'}, use_global_device_ids=true, to_apply=%region_4.8 | all-reduce | flops 4096 | bytes 32768 | tf_op jit(solution)/shard_map/psum | solution.py:103
  201.7 0.7 copy.26
  (90 shorter events, 14.5 us)
Async XLA Ops:
  0.6 10.8 %copy-start = (bf16[32,128,128]{2,1,0:T(8,128)(2,1)S(1)}, bf16[32,128,128]{2,1,0:T(8,128)(2,1)}, u32[]{:S(2)}) copy-start(bf16[32,128,128]{2,1,0:T(8,128)(2,1)} %param.13) | copy-start | bytes 3145732
  2.4 13.1 %collective-permute-start = (bf16[64,8,128]{2,1,0:T(8,128)(2,1)S(1)}, bf16[64,8,128]{2,1,0:T(8,128)(2,1)S(1)}, u32[]{:S(2)}, u32[]{:S(2)}) collective-permute-start(bf16[64,8,128]{2,1,0:T(8,128)(2,1)S(1)} %bitcast.141), channel_id=1, source_target_pairs={{2,0},{4,2},{6,4},{8,6},{10,8},{12,10},{14,12},{16,14},{18,16},{20... | collective-permute-start | bytes 393224 | tf_op jit(solution)/shard_map/ppermute | solution.py:15
  10.1 0.7 copy-start.10
  10.7 4.8 %copy-start.3 = (f32[32]{0:T(128)}, f32[32]{0:T(128)S(1)}, u32[]{:S(2)}) copy-start(f32[32]{0:T(128)S(1)} %compare_convert_fusion) | copy-start | bytes 388
  10.7 0.7 copy-start.15
  12.2 1.3 copy-start.1
  13.5 8.6 %collective-permute-start.1 = (bf16[64,8,128]{2,1,0:T(8,128)(2,1)S(1)}, bf16[64,8,128]{2,1,0:T(8,128)(2,1)S(1)}, u32[]{:S(2)}, u32[]{:S(2)}) collective-permute-start(bf16[64,8,128]{2,1,0:T(8,128)(2,1)S(1)} %fusion.3), channel_id=1, source_target_pairs={{30,0},{0,2},{2,4},{4,6},{6,8},{8,10},{10,12},{12,14},{14,16},{16,... | collective-permute-start | bytes 393224 | tf_op jit(solution)/shard_map/ppermute | solution.py:15
  13.6 1.3 copy-start.14
  13.6 2.6 %collective-permute-start.2 = (bf16[64,1024]{1,0:T(8,128)(2,1)S(1)}, bf16[64,1024]{1,0:T(8,128)(2,1)S(1)}, u32[]{:S(2)}, u32[]{:S(2)}) collective-permute-start(bf16[64,1024]{1,0:T(8,128)(2,1)S(1)} %multiply_convert_fusion.2), channel_id=1, source_target_pairs={{0,1},{1,0},{2,3},{3,2},{4,5},{5,4},{6,7},{7,6},{8,9},{9,8},{10,11... | collective-permute-start | bytes 393224 | tf_op jit(solution)/shard_map/ppermute | solution.py:19
  24.0 0.7 copy-start.7
  75.9 0.7 copy-start.4
  75.9 0.7 copy-start.11
  76.9 6.8 %collective-permute-start.3 = (bf16[64,8,128]{2,1,0:T(8,128)(2,1)S(1)}, bf16[64,8,128]{2,1,0:T(8,128)(2,1)S(1)}, u32[]{:S(2)}, u32[]{:S(2)}) collective-permute-start(bf16[64,8,128]{2,1,0:T(8,128)(2,1)S(1)} %bitcast.148), channel_id=1, source_target_pairs={{2,0},{4,2},{6,4},{8,6},{10,8},{12,10},{14,12},{16,14},{18,16},{20... | collective-permute-start | bytes 393224 | tf_op jit(solution)/shard_map/ppermute | solution.py:15
  80.2 4.3 %collective-permute-start.5 = (bf16[64,1024]{1,0:T(8,128)(2,1)S(1)}, bf16[64,1024]{1,0:T(8,128)(2,1)S(1)}, u32[]{:S(2)}, u32[]{:S(2)}) collective-permute-start(bf16[64,1024]{1,0:T(8,128)(2,1)S(1)} %get-tuple-element.7), channel_id=1, source_target_pairs={{0,1},{1,0},{2,3},{3,2},{4,5},{5,4},{6,7},{7,6},{8,9},{9,8},{10,11... | collective-permute-start | bytes 393224 | tf_op jit(solution)/shard_map/ppermute | solution.py:19
  82.2 1.5 copy-start.16
  82.2 9.7 %collective-permute-start.4 = (bf16[64,8,128]{2,1,0:T(8,128)(2,1)S(1)}, bf16[64,8,128]{2,1,0:T(8,128)(2,1)S(1)}, u32[]{:S(2)}, u32[]{:S(2)}) collective-permute-start(bf16[64,8,128]{2,1,0:T(8,128)(2,1)S(1)} %fusion.4), channel_id=1, source_target_pairs={{30,0},{0,2},{2,4},{4,6},{6,8},{8,10},{10,12},{12,14},{14,16},{16,... | collective-permute-start | bytes 393224 | tf_op jit(solution)/shard_map/ppermute | solution.py:15
  93.9 0.7 copy-start.8
  145.3 18.3 %copy-start.2 = (f32[64,1024]{1,0:T(8,128)}, f32[64,1024]{1,0:T(8,128)S(1)}, u32[]{:S(2)}) copy-start(f32[64,1024]{1,0:T(8,128)S(1)} %get-tuple-element.10) | copy-start | bytes 786436
  145.3 0.7 copy-start.5
  145.3 0.7 copy-start.12
  146.4 7.7 %collective-permute-start.6 = (bf16[64,8,128]{2,1,0:T(8,128)(2,1)S(1)}, bf16[64,8,128]{2,1,0:T(8,128)(2,1)S(1)}, u32[]{:S(2)}, u32[]{:S(2)}) collective-permute-start(bf16[64,8,128]{2,1,0:T(8,128)(2,1)S(1)} %bitcast.145), channel_id=1, source_target_pairs={{2,0},{4,2},{6,4},{8,6},{10,8},{12,10},{14,12},{16,14},{18,16},{20... | collective-permute-start | bytes 393224 | tf_op jit(solution)/shard_map/ppermute | solution.py:15
  150.5 4.4 %collective-permute-start.8 = (bf16[64,1024]{1,0:T(8,128)(2,1)S(1)}, bf16[64,1024]{1,0:T(8,128)(2,1)S(1)}, u32[]{:S(2)}, u32[]{:S(2)}) collective-permute-start(bf16[64,1024]{1,0:T(8,128)(2,1)S(1)} %get-tuple-element.9), channel_id=1, source_target_pairs={{0,1},{1,0},{2,3},{3,2},{4,5},{5,4},{6,7},{7,6},{8,9},{9,8},{10,11... | collective-permute-start | bytes 393224 | tf_op jit(solution)/shard_map/ppermute | solution.py:19
  152.6 1.6 copy-start.17
  152.6 9.8 %collective-permute-start.7 = (bf16[64,8,128]{2,1,0:T(8,128)(2,1)S(1)}, bf16[64,8,128]{2,1,0:T(8,128)(2,1)S(1)}, u32[]{:S(2)}, u32[]{:S(2)}) collective-permute-start(bf16[64,8,128]{2,1,0:T(8,128)(2,1)S(1)} %fusion.5), channel_id=1, source_target_pairs={{30,0},{0,2},{2,4},{4,6},{6,8},{8,10},{10,12},{12,14},{14,16},{16,... | collective-permute-start | bytes 393224 | tf_op jit(solution)/shard_map/ppermute | solution.py:15
  158.3 4.1 %copy-start.6 = (f32[32]{0:T(128)S(1)}, f32[32]{0:T(128)}, u32[]{:S(2)}) copy-start(f32[32]{0:T(128)} %copy-done.3) | copy-start | bytes 388
  158.3 4.1 %copy-start.13 = (s32[32]{0:T(128)S(1)}, s32[32]{0:T(128)}, u32[]{:S(2)}) copy-start(s32[32]{0:T(128)} %param.14) | copy-start | bytes 388
  163.6 0.7 copy-start.9
where the time goes:
time: 204 us; the launch traced here: 202 us
  blocking collectives  112 us (55%)
  other arithmetic  26.5 us (13%)
  matrix products  20.7 us (10%)
  local copies, waits for them, and re-layouts  15.8 us (8%)
  starting transfers between devices  15 us (7%)
  waiting for transfers between devices  10.2 us (5%)
    psum x2, blocking collectives, shards(): gram_matrix = lax.psum(local_gram, ('blk', 'scale')) / node_total  75.3 us
    psum x1, blocking collectives, shards(): rayleigh = lax.psum(local_projection, ('blk', 'scale')) / node_total  37 us
    ppermute x6, starting transfers between devices, from_behind(): return lax.ppermute(block, axis, route)  14.9 us
    another operation x6, other arithmetic, shards(): factor = jnp.linalg.cholesky(gram_matrix)  13 us
    dot_general x9, matrix products, place_rows(): jnp.einsum('cr,ckj->krj', onehot, partial_terms, precision=FULL_PRECISION)  12.5 us
    another operation x4, other arithmetic, shards(): jax.scipy.linalg.solve_triangular(factor, jnp.eye(vector_count, dtype=jnp...  11.1 us
    ppermute x6, waiting for transfers between devices, from_behind(): return lax.ppermute(block, axis, route)  10.2 us
    gather x6, local copies, waits for them, and re-layouts, apply_operator(): crossed = jnp.take(partner_vectors, partner, axis=1).astype(jnp.float32)  10 us
  transfers between devices with their start and end apart: 9, of which 3 were waited for; matrix products, arithmetic and copies ran while one was open for 12% of the time, Pallas kernels for 0%

commit v1 on v0

v1 whole, which is shorter than its diff:
```python
import functools

import jax
import jax.numpy as jnp
from jax import lax
from jax.experimental import pallas as pl
from jax.experimental.pallas import tpu as pltpu
from jax.sharding import PartitionSpec as P

ITERS = 2
BLOCK = 128
CROSS = 2
PANEL = 8
MESH = pl.DeviceIdType.MESH
FULL = lax.Precision.HIGHEST


def group_stages(total):
    stages, stride = [], 1
    while stride < total:
        size = min(8, total // stride)
        stages.append((stride, size))
        stride *= size
    return stages


def prepare(
    column_ref, target_ref, count_ref, blocks_ref, partner_ref,
    high_ref, low_ref, pair_ref, back_ref, turned_ref, aim_ref, dense,
):
    nodes = dense.shape[0]
    dense[...] = jnp.zeros_like(dense)
    back_ref[...] = jnp.zeros_like(back_ref)

    def spot(index):
        return pl.ds(pl.multiple_of(index * BLOCK, BLOCK), BLOCK)

    for slot in range(CROSS):
        weight = blocks_ref[slot]
        rows = pl.ds(slot * BLOCK, BLOCK)
        back_ref[rows, spot(column_ref[slot])] = weight
        turned_ref[rows, :] = weight.astype(jnp.float32).T.astype(jnp.bfloat16)
        aim_ref[slot, 0] = jnp.full((8, BLOCK), target_ref[slot] - nodes // BLOCK, jnp.int32)
        aim_ref[slot, 1] = jnp.full((8, BLOCK), column_ref[slot], jnp.int32)

    def place(slot, carry):
        weight = blocks_ref[slot].astype(jnp.float32)
        rows, columns = spot(target_ref[slot]), spot(column_ref[slot])
        dense[rows, columns] += weight
        dense[columns, rows] += weight.T
        return carry

    lax.fori_loop(CROSS, count_ref[0], place, 0)
    high = dense[...].astype(jnp.bfloat16)
    high_ref[...] = high
    low_ref[...] = (dense[...] - high.astype(jnp.float32)).astype(jnp.bfloat16)
    index = lax.broadcasted_iota(jnp.int32, (nodes, nodes), 0)
    pair_ref[...] = (index == partner_ref[...]).astype(jnp.float32).astype(jnp.bfloat16)


def inverse_factor(gram):
    size = gram.shape[0]
    rows = lax.broadcasted_iota(jnp.int32, (size, size), 0)
    columns = lax.broadcasted_iota(jnp.int32, (size, size), 1)
    whole = jnp.concatenate([gram, (rows == columns).astype(jnp.float32)], axis=1)
    width = 2 * size
    place = lax.broadcasted_iota(jnp.int32, (size, width), 0)

    def eliminate(panel, whole):
        active = place < size - PANEL * panel
        strips = [jnp.broadcast_to(whole[:, k : k + 1], (size, width)) for k in range(PANEL)]
        pivots = []
        for j in range(PANEL):
            pivot = strips[j][j : j + 1, :]
            pivots.append(pivot)
            factor = jnp.where(active & (place > j), strips[j] * (1.0 / pivot), 0.0)
            for k in range(j + 1, PANEL):
                strips[k] = strips[k] - factor * strips[k][j : j + 1, :]
            whole = whole - factor * whole[j : j + 1, :]
        done = whole[:PANEL] * (1.0 / jnp.sqrt(jnp.concatenate(pivots, axis=0)))
        whole = jnp.concatenate([whole[PANEL:], done], axis=0)
        return pltpu.roll(whole, width - PANEL, 1)

    return lax.fori_loop(0, size // PANEL, eliminate, whole)[:, :size]


def iterate(
    blk_total, scale_total,
    start_ref, degree_ref, high_ref, low_ref, pair_ref, back_ref, turned_ref, aim_ref,
    subspace_ref, rayleigh_ref,
    scaled_buf, partner_buf, ahead_out, behind_out, ahead_in, behind_in,
    turned_in, aim_in, forward_weights, *rest,
):
    stages = group_stages(blk_total * scale_total)
    gather_bufs = rest[: len(stages)]
    pair_send, pair_recv, edge_send, edge_recv, gather_send, gather_recv = rest[len(stages):]
    vectors, nodes = start_ref.shape
    row_blocks = nodes // BLOCK
    node_total = nodes * blk_total * scale_total
    blk, scale = lax.axis_index("blk"), lax.axis_index("scale")
    me = blk * scale_total + scale
    ahead = ((blk + 1) % blk_total, scale)
    behind = ((blk + blk_total - 1) % blk_total, scale)
    partner = (blk, scale + 1 - 2 * (scale % 2))

    def peer(stride, size, shift):
        digit = (me // stride) % size
        other = (digit + shift) % size
        place = me + (other - digit) * stride
        return other, (place // scale_total, place % scale_total)

    barrier = pltpu.get_barrier_semaphore()
    greeted = [ahead, behind]
    for stride, size in stages:
        greeted += [peer(stride, size, shift)[1] for shift in range(1, size)]
    for device in greeted:
        pl.semaphore_signal(barrier, inc=1, device_id=device, device_id_type=MESH)

    inv_sqrt_degree = 1.0 / jnp.sqrt(degree_ref[...].astype(jnp.float32))
    sent = []

    def send(source, target, send_sem, recv_sem, device):
        copy = pltpu.make_async_remote_copy(
            src_ref=source, dst_ref=target, send_sem=send_sem, recv_sem=recv_sem,
            device_id=device, device_id_type=MESH,
        )
        copy.start()
        sent.append(copy)
        return copy

    def chosen(values, marks):
        picked = jnp.zeros((vectors, BLOCK), jnp.float32)
        mark = jnp.broadcast_to(marks[:1, :], (vectors, BLOCK))
        for r in range(row_blocks):
            picked = jnp.where(mark == r, values[:, r * BLOCK : (r + 1) * BLOCK], picked)
        return picked.astype(jnp.bfloat16)

    def product(left, right):
        return jnp.dot(left, right, preferred_element_type=jnp.float32)

    def operate(step, current):
        scaled = (current * inv_sqrt_degree).astype(jnp.bfloat16)
        scaled_buf[step] = scaled
        if step == 0:
            pl.semaphore_wait(barrier, len(greeted))
            weights_copy = send(turned_ref, turned_in, edge_send.at[6], edge_recv.at[6], ahead)
            aim_copy = send(aim_ref, aim_in, edge_send.at[7], edge_recv.at[7], ahead)
        pair_copy = send(
            scaled_buf.at[step], partner_buf.at[step], pair_send.at[step], pair_recv.at[step], partner
        )
        wide = scaled.astype(jnp.float32)
        for slot in range(CROSS):
            ahead_out[step, :, slot * BLOCK : (slot + 1) * BLOCK] = chosen(wide, aim_ref[slot, 1])
        ahead_copy = send(
            ahead_out.at[step], behind_in.at[step], edge_send.at[2 * step], edge_recv.at[2 * step], ahead
        )
        if step == 0:
            weights_copy.wait_recv()
            aim_copy.wait_recv()
            for slot in range(CROSS):
                span = slice(slot * BLOCK, (slot + 1) * BLOCK)
                weight = turned_in[span, :].astype(jnp.float32)
                mark = jnp.broadcast_to(aim_in[slot, 0][:1, :], (BLOCK, BLOCK))
                for r in range(row_blocks):
                    forward_weights[span, r * BLOCK : (r + 1) * BLOCK] = jnp.where(
                        mark == r, weight, 0.0
                    ).astype(jnp.bfloat16)
        for slot in range(CROSS):
            behind_out[step, :, slot * BLOCK : (slot + 1) * BLOCK] = chosen(wide, aim_in[slot, 0])
        behind_copy = send(
            behind_out.at[step], ahead_in.at[step],
            edge_send.at[2 * step + 1], edge_recv.at[2 * step + 1], behind,
        )
        total = product(scaled, high_ref[...]) + product(scaled, low_ref[...])
        pair_copy.wait_recv()
        total += product(partner_buf[step], pair_ref[...])
        ahead_copy.wait_recv()
        total += product(behind_in[step], forward_weights[...])
        behind_copy.wait_recv()
        total += product(ahead_in[step], back_ref[...])
        return current + inv_sqrt_degree * total

    def over_devices(step, local):
        half = vectors // 2
        value = jnp.concatenate([local[:half], local[half:]], axis=1)
        slot_base = 0
        for (stride, size), buf in zip(stages, gather_bufs):
            digit = (me // stride) % size
            buf[step, digit] = value
            copies = []
            for shift in range(1, size):
                other, device = peer(stride, size, shift)
                copies.append(send(
                    buf.at[step, digit], buf.at[step, digit],
                    gather_send.at[step, slot_base + shift], gather_recv.at[step, slot_base + digit],
                    device,
                ))
            for shift in range(1, size):
                other, device = peer(stride, size, shift)
                pltpu.make_async_remote_copy(
                    src_ref=buf.at[step, digit], dst_ref=buf.at[step, other],
                    send_sem=gather_send.at[step, slot_base + shift],
                    recv_sem=gather_recv.at[step, slot_base + other],
                    device_id=device, device_id_type=MESH,
                ).wait_recv()
            value = buf[step, 0]
            for other in range(1, size):
                value = value + buf[step, other]
            slot_base += size
        return jnp.concatenate([value[:, :vectors], value[:, vectors:]], axis=0) / node_total

    def inner(left, right):
        return lax.dot_general(
            left, right, (((1,), (1,)), ((), ())), precision=FULL, preferred_element_type=jnp.float32
        )

    subspace = start_ref[...]
    for step in range(ITERS):
        images = operate(step, subspace)
        gram = over_devices(step, inner(images, images))
        subspace = jnp.dot(
            inverse_factor(gram), images, precision=FULL, preferred_element_type=jnp.float32
        )
    subspace_ref[...] = subspace
    images = operate(ITERS, subspace)
    rayleigh_ref[...] = over_devices(ITERS, inner(subspace, images))
    for copy in sent:
        copy.wait_send()


def solution(mesh):
    blk_total, scale_total = mesh.shape["blk"], mesh.shape["scale"]
    stages = group_stages(blk_total * scale_total)

    def shards(start_block, blocks, block_column, block_target, block_count, partner, degree):
        vectors, nodes = start_block.shape
        vmem = pl.BlockSpec(memory_space=pltpu.VMEM)
        smem = pl.BlockSpec(memory_space=pltpu.SMEM)
        half = jnp.bfloat16
        prepared = pl.pallas_call(
            prepare,
            out_shape=(
                jax.ShapeDtypeStruct((nodes, nodes), half),
                jax.ShapeDtypeStruct((nodes, nodes), half),
                jax.ShapeDtypeStruct((nodes, nodes), half),
                jax.ShapeDtypeStruct((CROSS * BLOCK, nodes), half),
                jax.ShapeDtypeStruct((CROSS * BLOCK, BLOCK), half),
                jax.ShapeDtypeStruct((CROSS, 2, 8, BLOCK), jnp.int32),
            ),
            in_specs=[smem, smem, smem, vmem, vmem],
            out_specs=(vmem,) * 6,
            scratch_shapes=[pltpu.VMEM((nodes, nodes), jnp.float32)],
            compiler_params=pltpu.CompilerParams(vmem_limit_bytes=32 * 2**20),
        )(block_column, block_target, block_count, blocks, partner.reshape(1, nodes))
        steps = ITERS + 1
        edge = pltpu.VMEM((steps, vectors, CROSS * BLOCK), half)
        counts = sum(size for _, size in stages)
        return pl.pallas_call(
            functools.partial(iterate, blk_total, scale_total),
            out_shape=(
                jax.ShapeDtypeStruct((vectors, nodes), jnp.float32),
                jax.ShapeDtypeStruct((vectors, vectors), jnp.float32),
            ),
            in_specs=[vmem] * 8,
            out_specs=(vmem, vmem),
            scratch_shapes=[
                pltpu.VMEM((steps, vectors, nodes), half),
                pltpu.VMEM((steps, vectors, nodes), half),
                edge, edge, edge, edge,
                pltpu.VMEM((CROSS * BLOCK, BLOCK), half),
                pltpu.VMEM((CROSS, 2, 8, BLOCK), jnp.int32),
                pltpu.VMEM((CROSS * BLOCK, nodes), half),
                *[
                    pltpu.VMEM((steps, size, vectors // 2, 2 * vectors), jnp.float32)
                    for _, size in stages
                ],
                pltpu.SemaphoreType.DMA((steps,)),
                pltpu.SemaphoreType.DMA((steps,)),
                pltpu.SemaphoreType.DMA((2 * steps + 2,)),
                pltpu.SemaphoreType.DMA((2 * steps + 2,)),
                pltpu.SemaphoreType.DMA((steps, counts)),
                pltpu.SemaphoreType.DMA((steps, counts)),
            ],
            compiler_params=pltpu.CompilerParams(
                collective_id=0, has_side_effects=True, vmem_limit_bytes=40 * 2**20
            ),
        )(start_block, degree.reshape(1, nodes), *prepared)

    return jax.shard_map(
        shards,
        mesh=mesh,
        in_specs=(
            P(None, ("blk", "scale")),
            P(("blk", "scale"), None, None),
            P(("blk", "scale")),
            P(("blk", "scale")),
            P(("blk", "scale")),
            P(("blk", "scale")),
            P(("blk", "scale")),
        ),
        out_specs=(P(None, ("blk", "scale")), P()),
        check_vma=False,
    )
```

time: 204 us -> 66.7 us (0.33)
  blocking collectives: 112 us -> 0 us
  Pallas kernels: 0 us -> 58.8 us
  other arithmetic: 26.5 us -> 0 us
  matrix products: 20.7 us -> 0 us
  starting transfers between devices: 15 us -> 0 us
  waiting for transfers between devices: 10.2 us -> 0 us
  local copies, waits for them, and re-layouts: 15.8 us -> 6.16 us
    psum x3 -> x0, blocking collectives: 112 us -> none  [the longest x2 75.3 us: shards(): gram_matrix = lax.psum(local_gram, ('blk', 'scale')) / node_total]
    pallas_call x0 -> x2, Pallas kernels: none -> 58.8 us  [the longest x1 56.8 us: shards(): pl.pallas_call(functools.partial(iterate, blk_total, scale_total), out_sh...]
    another operation x10 -> x0, other arithmetic: 24.1 us -> none  [the longest x6 13 us: shards(): factor = jnp.linalg.cholesky(gram_matrix)]
    dot_general x26 -> x0, matrix products: 20.2 us -> none  [the longest x9 12.5 us: place_rows(): jnp.einsum('cr,ckj->krj', onehot, partial_terms, precision=FULL_PRECISION)]
    ppermute x9 -> x0, starting transfers between devices: 15 us -> none  [the longest x6 14.9 us: from_behind(): return lax.ppermute(block, axis, route)]
    ppermute x9 -> x0, waiting for transfers between devices: 10.2 us -> none  [the longest x6 10.2 us: from_behind(): return lax.ppermute(block, axis, route)]
    gather x6 -> x0, local copies, waits for them, and re-layouts: 10 us -> none  [apply_operator(): crossed = jnp.take(partner_vectors, partner, axis=1).astype(jnp.float32)]
    unnamed x40 -> x14, local copies, waits for them, and re-layouts: 5.13 us -> 6.16 us
  transfers between devices with their start and end apart: 9 -> 0, of which waited for: 3 -> 0; matrix products, arithmetic and copies ran while one was open for 12% -> 0% of each run, Pallas kernels for 0% -> 0%
where the time goes in v1:
time: 66.7 us; the launch traced here: 66.2 us
  Pallas kernels  58.8 us (88%)
  local copies, waits for them, and re-layouts  6.16 us (9%)
  between operations  1.31 us (2%)
    pallas_call x1, Pallas kernels, shards(): pl.pallas_call(functools.partial(iterate, blk_total, scale_total), out_sh...  56.8 us
    unnamed x14, local copies, waits for them, and re-layouts  6.16 us
    pallas_call x1, Pallas kernels, shards(): pl.pallas_call(prepare, out_shape=(jax.ShapeDtypeStruct((nodes, nodes), h...  1.93 us

profile of v1, /device:TPU:0, one launch (start us, length us, event | category | flops | bytes accessed | tf_op | source)
XLA Modules:
  0.0 66.2 jit_solution(7199471311710050496)
XLA Ops:
  1.3 0.0 copy-start
  1.3 1.2 %copy-done = bf16[32,128,128]{2,1,0:T(8,128)(2,1)S(1)} copy-done((bf16[32,128,128]{2,1,0:T(8,128)(2,1)S(1)}, bf16[32,128,128]{2,1,0:T(8,128)(2,1)}, u32[]{:S(2)}) %copy-start) | copy-done | bytes 1048600
  2.5 0.0 copy-start.2
  2.5 0.7 %copy-done.2 = s32[1024]{0:T(1024)S(1)} copy-done((s32[1024]{0:T(1024)S(1)}, s32[1024]{0:T(1024)}, u32[]{:S(2)}) %copy-start.2) | copy-done | bytes 4120
  3.2 0.0 copy-start.4
  3.2 0.7 copy-done.4
  3.8 0.0 copy-start.5
  3.8 0.7 copy-done.5
  4.5 1.9 %shard_map.86 = (bf16[1024,1024]{1,0:T(8,128)(2,1)S(1)}, bf16[1024,1024]{1,0:T(8,128)(2,1)S(1)}, bf16[1024,1024]{1,0:T(8,128)(2,1)S(1)}, bf16[256,1024]{1,0:T(8,...) custom-call(s32[32]{0:T(128)S(1)} %copy-done.4, s32[32]{0:T(128)S(1)} %copy-done.5, ...), custom_call_target="tpu_custom_call" | custom-call | tf_op jit(solution)/shard_map/pallas_call | solution.py:240
  6.4 0.0 copy-start.1
  6.4 0.9 %copy-done.1 = f32[64,1024]{1,0:T(8,128)S(1)} copy-done((f32[64,1024]{1,0:T(8,128)S(1)}, f32[64,1024]{1,0:T(8,128)}, u32[]{:S(2)}) %copy-start.1) | copy-done | bytes 262168
  7.4 0.0 copy-start.3
  7.4 0.7 %copy-done.3 = s32[1024]{0:T(1024)S(1)} copy-done((s32[1024]{0:T(1024)S(1)}, s32[1024]{0:T(1024)}, u32[]{:S(2)}) %copy-start.3) | copy-done | bytes 4120
  8.1 56.8 %shard_map.87 = (f32[64,1024]{1,0:T(8,128)S(1)}, f32[64,64]{1,0:T(8,128)S(1)}) custom-call(f32[64,1024]{1,0:T(8,128)S(1)} %copy-done.1, s32[1,1024]{1,0:T(1,128)S(1)} %bitcast.3, bf16[1024,1024]{1,0:T(8,128)(2,1)S(1)} %get-tuple-element.8.high_ref, bf16[1024,1024]{1,0:T(8,128)(2,1)S(1)} %get-tuple-element.9.low_ref, ...), custom_call_target="tpu_custom_call" | custom-call | tf_op jit(solution)/shard_map/pallas_call | solution.py:258
  64.9 0.7 %copy.12 = f32[64,1024]{1,0:T(8,128)} copy(f32[64,1024]{1,0:T(8,128)S(1)} %get-tuple-element.16) | data formatting | bytes 524288
  65.6 0.6 copy.13
Async XLA Ops:
  1.3 1.2 %copy-start = (bf16[32,128,128]{2,1,0:T(8,128)(2,1)S(1)}, bf16[32,128,128]{2,1,0:T(8,128)(2,1)}, u32[]{:S(2)}) copy-start(bf16[32,128,128]{2,1,0:T(8,128)(2,1)} %blocks_ref.1) | copy-start | bytes 3145732
  2.5 0.7 %copy-start.2 = (s32[1024]{0:T(1024)S(1)}, s32[1024]{0:T(1024)}, u32[]{:S(2)}) copy-start(s32[1024]{0:T(1024)} %param.12) | copy-start | bytes 12292
  3.2 0.7 copy-start.4
  3.8 0.7 copy-start.5
  6.4 1.0 %copy-start.1 = (f32[64,1024]{1,0:T(8,128)S(1)}, f32[64,1024]{1,0:T(8,128)}, u32[]{:S(2)}) copy-start(f32[64,1024]{1,0:T(8,128)} %start_ref.1) | copy-start | bytes 786436
  7.4 0.7 %copy-start.3 = (s32[1024]{0:T(1024)S(1)}, s32[1024]{0:T(1024)}, u32[]{:S(2)}) copy-start(s32[1024]{0:T(1024)} %param.13) | copy-start | bytes 12292

commit v2 on v1

--- a/solution.py
+++ b/solution.py
@@ -7,7 +7,7 @@
 from jax.experimental.pallas import tpu as pltpu
 from jax.sharding import PartitionSpec as P
 
-ITERS = 2
+STEPS = 3
 BLOCK = 128
 CROSS = 2
 PANEL = 8
@@ -129,8 +129,9 @@
         return copy
 
     def chosen(values, marks):
-        picked = jnp.zeros((vectors, BLOCK), jnp.float32)
-        mark = jnp.broadcast_to(marks[:1, :], (vectors, BLOCK))
+        height = values.shape[0]
+        picked = jnp.zeros((height, BLOCK), jnp.float32)
+        mark = jnp.broadcast_to(marks[:1, :], (height, BLOCK))
         for r in range(row_blocks):
             picked = jnp.where(mark == r, values[:, r * BLOCK : (r + 1) * BLOCK], picked)
         return picked.astype(jnp.bfloat16)
@@ -138,25 +139,42 @@
     def product(left, right):
         return jnp.dot(left, right, preferred_element_type=jnp.float32)
 
-    def operate(step, current):
-        scaled = (current * inv_sqrt_degree).astype(jnp.bfloat16)
-        scaled_buf[step] = scaled
+    def depart(step, current):
+        exact = current * inv_sqrt_degree
+        scaled = exact.astype(jnp.bfloat16)
+        wide = scaled.astype(jnp.float32)
+        if step > 0:
+            wide = jnp.concatenate([wide, exact - wide], axis=0)
+            scaled = wide.astype(jnp.bfloat16)
+        height = wide.shape[0]
+        rows = pl.ds(0, height)
+        scaled_buf[step, :height] = scaled
+        for slot in range(CROSS):
+            span = slice(slot * BLOCK, (slot + 1) * BLOCK)
+            ahead_out[step, :height, span] = chosen(wide, aim_ref[slot, 1])
         if step == 0:
             pl.semaphore_wait(barrier, len(greeted))
             weights_copy = send(turned_ref, turned_in, edge_send.at[6], edge_recv.at[6], ahead)
             aim_copy = send(aim_ref, aim_in, edge_send.at[7], edge_recv.at[7], ahead)
+        ahead_copy = send(
+            ahead_out.at[step, rows], behind_in.at[step, rows],
+            edge_send.at[2 * step], edge_recv.at[2 * step], ahead,
+        )
         pair_copy = send(
-            scaled_buf.at[step], partner_buf.at[step], pair_send.at[step], pair_recv.at[step], partner
-        )
-        wide = scaled.astype(jnp.float32)
+            scaled_buf.at[step, rows], partner_buf.at[step, rows],
+            pair_send.at[step], pair_recv.at[step], partner,
+        )
+        if step == 0:
+            aim_copy.wait_recv()
         for slot in range(CROSS):
-            ahead_out[step, :, slot * BLOCK : (slot + 1) * BLOCK] = chosen(wide, aim_ref[slot, 1])
-        ahead_copy = send(
-            ahead_out.at[step], behind_in.at[step], edge_send.at[2 * step], edge_recv.at[2 * step], ahead
+            span = slice(slot * BLOCK, (slot + 1) * BLOCK)
+            behind_out[step, :height, span] = chosen(wide, aim_in[slot, 0])
+        behind_copy = send(
+            behind_out.at[step, rows], ahead_in.at[step, rows],
+            edge_send.at[2 * step + 1], edge_recv.at[2 * step + 1], behind,
         )
         if step == 0:
             weights_copy.wait_recv()
-            aim_copy.wait_recv()
             for slot in range(CROSS):
                 span = slice(slot * BLOCK, (slot + 1) * BLOCK)
                 weight = turned_in[span, :].astype(jnp.float32)
@@ -165,48 +183,63 @@
                     forward_weights[span, r * BLOCK : (r + 1) * BLOCK] = jnp.where(
                         mark == r, weight, 0.0
                     ).astype(jnp.bfloat16)
-        for slot in range(CROSS):
-            behind_out[step, :, slot * BLOCK : (slot + 1) * BLOCK] = chosen(wide, aim_in[slot, 0])
-        behind_copy = send(
-            behind_out.at[step], ahead_in.at[step],
-            edge_send.at[2 * step + 1], edge_recv.at[2 * step + 1], behind,
-        )
-        total = product(scaled, high_ref[...]) + product(scaled, low_ref[...])
+        return height, scaled, pair_copy, ahead_copy, behind_copy
+
+    def nearby(trip):
+        return product(trip[1], high_ref[...]) + product(trip[1], low_ref[...])
+
+    def arrive(step, current, trip, total):
+        height, _, pair_copy, ahead_copy, behind_copy = trip
         pair_copy.wait_recv()
-        total += product(partner_buf[step], pair_ref[...])
+        total += product(partner_buf[step, :height], pair_ref[...])
         ahead_copy.wait_recv()
-        total += product(behind_in[step], forward_weights[...])
+        total += product(behind_in[step, :height], forward_weights[...])
         behind_copy.wait_recv()
-        total += product(ahead_in[step], back_ref[...])
+        total += product(ahead_in[step, :height], back_ref[...])
+        if height > vectors:
+            total = total[:vectors] + total[vectors:]
         return current + inv_sqrt_degree * total
 
-    def over_devices(step, local):
+    bases = [sum(size for _, size in stages[:level]) for level in range(len(stages))]
+
+    def share(which, level, value):
+        (stride, size), buf, base = stages[level], gather_bufs[level], bases[level]
+        digit = (me // stride) % size
+        buf[which, digit] = value
+        for shift in range(1, size):
+            send(
+                buf.at[which, digit], buf.at[which, digit],
+                gather_send.at[which, base + shift], gather_recv.at[which, base + digit],
+                peer(stride, size, shift)[1],
+            )
+
+    def collect(which, level):
+        (stride, size), buf, base = stages[level], gather_bufs[level], bases[level]
+        digit = (me // stride) % size
+        for shift in range(1, size):
+            other, device = peer(stride, size, shift)
+            pltpu.make_async_remote_copy(
+                src_ref=buf.at[which, digit], dst_ref=buf.at[which, other],
+                send_sem=gather_send.at[which, base + shift],
+                recv_sem=gather_recv.at[which, base + other],
+                device_id=device, device_id_type=MESH,
+            ).wait_recv()
+        value = buf[which, 0]
+        for other in range(1, size):
+            value = value + buf[which, other]
+        return value
+
+    def advance(which, level):
+        value = collect(which, level)
+        if level + 1 < len(stages):
+            share(which, level + 1, value)
+        return value
+
+    def folded(value):
         half = vectors // 2
-        value = jnp.concatenate([local[:half], local[half:]], axis=1)
-        slot_base = 0
-        for (stride, size), buf in zip(stages, gather_bufs):
-            digit = (me // stride) % size
-            buf[step, digit] = value
-            copies = []
-            for shift in range(1, size):
-                other, device = peer(stride, size, shift)
-                copies.append(send(
-                    buf.at[step, digit], buf.at[step, digit],
-                    gather_send.at[step, slot_base + shift], gather_recv.at[step, slot_base + digit],
-                    device,
-                ))
-            for shift in range(1, size):
-                other, device = peer(stride, size, shift)
-                pltpu.make_async_remote_copy(
-                    src_ref=buf.at[step, digit], dst_ref=buf.at[step, other],
-                    send_sem=gather_send.at[step, slot_base + shift],
-                    recv_sem=gather_recv.at[step, slot_base + other],
-                    device_id=device, device_id_type=MESH,
-                ).wait_recv()
-            value = buf[step, 0]
-            for other in range(1, size):
-                value = value + buf[step, other]
-            slot_base += size
+        return jnp.concatenate([value[:half], value[half:]], axis=1)
+
+    def unfolded(value):
         return jnp.concatenate([value[:, :vectors], value[:, vectors:]], axis=0) / node_total
 
     def inner(left, right):
@@ -214,16 +247,35 @@
             left, right, (((1,), (1,)), ((), ())), precision=FULL, preferred_element_type=jnp.float32
         )
 
-    subspace = start_ref[...]
-    for step in range(ITERS):
-        images = operate(step, subspace)
-        gram = over_devices(step, inner(images, images))
-        subspace = jnp.dot(
-            inverse_factor(gram), images, precision=FULL, preferred_element_type=jnp.float32
-        )
-    subspace_ref[...] = subspace
-    images = operate(ITERS, subspace)
-    rayleigh_ref[...] = over_devices(ITERS, inner(subspace, images))
+    def full(left, right):
+        return jnp.dot(left, right, precision=FULL, preferred_element_type=jnp.float32)
+
+    last = len(stages) - 1
+    start = start_ref[...]
+    trip = depart(0, start)
+    first = arrive(0, start, trip, nearby(trip))
+    trip = depart(1, first)
+    share(0, 0, folded(inner(first, first)))
+    total = nearby(trip)
+    second = arrive(1, first, trip, total)
+    trip = depart(2, second)
+    advance(0, 0)
+    share(1, 0, folded(inner(second, second)))
+    total = nearby(trip)
+    third = arrive(2, second, trip, total)
+    share(2, 0, folded(inner(second, third)))
+    for level in range(1, last):
+        advance(0, level)
+    advance(1, 0)
+    first_inverse = inverse_factor(unfolded(collect(0, last)))
+    for level in range(last):
+        advance(2, level)
+        if level + 1 < last:
+            advance(1, level + 1)
+    middle = inner(full(first_inverse, unfolded(collect(1, last))), first_inverse)
+    change = full(inverse_factor(middle), first_inverse)
+    subspace_ref[...] = full(change, second)
+    rayleigh_ref[...] = inner(full(change, unfolded(collect(2, last))), change)
     for copy in sent:
         copy.wait_send()
 
@@ -252,8 +304,8 @@
             scratch_shapes=[pltpu.VMEM((nodes, nodes), jnp.float32)],
             compiler_params=pltpu.CompilerParams(vmem_limit_bytes=32 * 2**20),
         )(block_column, block_target, block_count, blocks, partner.reshape(1, nodes))
-        steps = ITERS + 1
-        edge = pltpu.VMEM((steps, vectors, CROSS * BLOCK), half)
+        steps = STEPS
+        edge = pltpu.VMEM((steps, 2 * vectors, CROSS * BLOCK), half)
         counts = sum(size for _, size in stages)
         return pl.pallas_call(
             functools.partial(iterate, blk_total, scale_total),
@@ -264,8 +316,8 @@
             in_specs=[vmem] * 8,
             out_specs=(vmem, vmem),
             scratch_shapes=[
-                pltpu.VMEM((steps, vectors, nodes), half),
-                pltpu.VMEM((steps, vectors, nodes), half),
+                pltpu.VMEM((steps, 2 * vectors, nodes), half),
+                pltpu.VMEM((steps, 2 * vectors, nodes), half),
                 edge, edge, edge, edge,
                 pltpu.VMEM((CROSS * BLOCK, BLOCK), half),
                 pltpu.VMEM((CROSS, 2, 8, BLOCK), jnp.int32),

time: 66.7 us -> 47.6 us (0.71)
  Pallas kernels: 58.8 us -> 39.8 us
    pallas_call x1, Pallas kernels: 56.8 us -> 37.8 us  [shards(): pl.pallas_call(functools.partial(iterate, blk_total, scale_total), out_sh...]
where the time goes in v2:
time: 47.6 us; the launch traced here: 47.3 us
  Pallas kernels  39.8 us (84%)
  local copies, waits for them, and re-layouts  6.16 us (13%)
  between operations  1.31 us (3%)
    pallas_call x1, Pallas kernels, shards(): pl.pallas_call(functools.partial(iterate, blk_total, scale_total), out_sh...  37.8 us
    unnamed x14, local copies, waits for them, and re-layouts  6.16 us
    pallas_call x1, Pallas kernels, shards(): pl.pallas_call(prepare, out_shape=(jax.ShapeDtypeStruct((nodes, nodes), h...  1.92 us

profile of v2, /device:TPU:0, one launch (start us, length us, event | category | flops | bytes accessed | tf_op | source)
XLA Modules:
  0.0 47.3 jit_solution(8378307595063263095)
XLA Ops:
  1.3 0.0 copy-start
  1.3 1.2 %copy-done = bf16[32,128,128]{2,1,0:T(8,128)(2,1)S(1)} copy-done((bf16[32,128,128]{2,1,0:T(8,128)(2,1)S(1)}, bf16[32,128,128]{2,1,0:T(8,128)(2,1)}, u32[]{:S(2)}) %copy-start) | copy-done | bytes 1048600
  2.5 0.0 copy-start.2
  2.5 0.7 %copy-done.2 = s32[1024]{0:T(1024)S(1)} copy-done((s32[1024]{0:T(1024)S(1)}, s32[1024]{0:T(1024)}, u32[]{:S(2)}) %copy-start.2) | copy-done | bytes 4120
  3.2 0.0 copy-start.4
  3.2 0.7 %copy-done.4 = s32[32]{0:T(128)S(1)} copy-done((s32[32]{0:T(128)S(1)}, s32[32]{0:T(128)}, u32[]{:S(2)}) %copy-start.4) | copy-done | bytes 152
  3.8 0.0 copy-start.5
  3.8 0.7 %copy-done.5 = s32[32]{0:T(128)S(1)} copy-done((s32[32]{0:T(128)S(1)}, s32[32]{0:T(128)}, u32[]{:S(2)}) %copy-start.5) | copy-done | bytes 152
  4.5 1.9 %shard_map.86 = (bf16[1024,1024]{1,0:T(8,128)(2,1)S(1)}, bf16[1024,1024]{1,0:T(8,128)(2,1)S(1)}, bf16[1024,1024]{1,0:T(8,128)(2,1)S(1)}, bf16[256,1024]{1,0:T(8,...) custom-call(s32[32]{0:T(128)S(1)} %copy-done.4, s32[32]{0:T(128)S(1)} %copy-done.5, ...), custom_call_target="tpu_custom_call" | custom-call | tf_op jit(solution)/shard_map/pallas_call | solution.py:292
  6.4 0.0 copy-start.1
  6.4 0.9 %copy-done.1 = f32[64,1024]{1,0:T(8,128)S(1)} copy-done((f32[64,1024]{1,0:T(8,128)S(1)}, f32[64,1024]{1,0:T(8,128)}, u32[]{:S(2)}) %copy-start.1) | copy-done | bytes 262168
  7.4 0.0 copy-start.3
  7.4 0.7 %copy-done.3 = s32[1024]{0:T(1024)S(1)} copy-done((s32[1024]{0:T(1024)S(1)}, s32[1024]{0:T(1024)}, u32[]{:S(2)}) %copy-start.3) | copy-done | bytes 4120
  8.1 37.8 %shard_map.87 = (f32[64,1024]{1,0:T(8,128)S(1)}, f32[64,64]{1,0:T(8,128)S(1)}) custom-call(f32[64,1024]{1,0:T(8,128)S(1)} %copy-done.1, s32[1,1024]{1,0:T(1,128)S(1)} %bitcast.3, bf16[1024,1024]{1,0:T(8,128)(2,1)S(1)} %get-tuple-element.8.high_ref, bf16[1024,1024]{1,0:T(8,128)(2,1)S(1)} %get-tuple-element.9.low_ref, ...), custom_call_target="tpu_custom_call" | custom-call | tf_op jit(solution)/shard_map/pallas_call | solution.py:310
  45.9 0.7 %copy.12 = f32[64,1024]{1,0:T(8,128)} copy(f32[64,1024]{1,0:T(8,128)S(1)} %get-tuple-element.16) | data formatting | bytes 524288
  46.6 0.6 %copy.13 = f32[64,64]{1,0:T(8,128)} copy(f32[64,64]{1,0:T(8,128)S(1)} %get-tuple-element.17) | data formatting | bytes 32768
Async XLA Ops:
  1.3 1.2 %copy-start = (bf16[32,128,128]{2,1,0:T(8,128)(2,1)S(1)}, bf16[32,128,128]{2,1,0:T(8,128)(2,1)}, u32[]{:S(2)}) copy-start(bf16[32,128,128]{2,1,0:T(8,128)(2,1)} %blocks_ref.1) | copy-start | bytes 3145732
  2.5 0.7 %copy-start.2 = (s32[1024]{0:T(1024)S(1)}, s32[1024]{0:T(1024)}, u32[]{:S(2)}) copy-start(s32[1024]{0:T(1024)} %param.12) | copy-start | bytes 12292
  3.2 0.7 %copy-start.4 = (s32[32]{0:T(128)S(1)}, s32[32]{0:T(128)}, u32[]{:S(2)}) copy-start(s32[32]{0:T(128)} %column_ref.1) | copy-start | bytes 388
  3.8 0.7 %copy-start.5 = (s32[32]{0:T(128)S(1)}, s32[32]{0:T(128)}, u32[]{:S(2)}) copy-start(s32[32]{0:T(128)} %target_ref.1) | copy-start | bytes 388
  6.4 1.0 %copy-start.1 = (f32[64,1024]{1,0:T(8,128)S(1)}, f32[64,1024]{1,0:T(8,128)}, u32[]{:S(2)}) copy-start(f32[64,1024]{1,0:T(8,128)} %start_ref.1) | copy-start | bytes 786436
  7.4 0.7 %copy-start.3 = (s32[1024]{0:T(1024)S(1)}, s32[1024]{0:T(1024)}, u32[]{:S(2)}) copy-start(s32[1024]{0:T(1024)} %param.13) | copy-start | bytes 12292

commit v3 on v2

--- a/solution.py
+++ b/solution.py
@@ -25,12 +25,26 @@
 
 
 def prepare(
-    column_ref, target_ref, count_ref, blocks_ref, partner_ref,
-    high_ref, low_ref, pair_ref, back_ref, turned_ref, aim_ref, dense,
+    count_ref, column_src, target_src, blocks_src, partner_src, start_src, degree_src,
+    dense, back_ref, turned_ref, aim_ref, partner_ref, start_ref, scale_ref,
+    column_ref, target_ref, blocks_ref, degree_ref, arrived,
 ):
     nodes = dense.shape[0]
+    pairs = (
+        (column_src, column_ref), (target_src, target_ref), (blocks_src, blocks_ref),
+        (partner_src, partner_ref), (start_src, start_ref), (degree_src, degree_ref),
+    )
+    copies = [
+        pltpu.make_async_copy(source, target, arrived.at[k])
+        for k, (source, target) in enumerate(pairs)
+    ]
+    for copy in copies:
+        copy.start()
     dense[...] = jnp.zeros_like(dense)
     back_ref[...] = jnp.zeros_like(back_ref)
+    for copy in copies:
+        copy.wait()
+    scale_ref[...] = 1.0 / jnp.sqrt(degree_ref[...].astype(jnp.float32))
 
     def spot(index):
         return pl.ds(pl.multiple_of(index * BLOCK, BLOCK), BLOCK)
@@ -51,11 +65,6 @@
         return carry
 
     lax.fori_loop(CROSS, count_ref[0], place, 0)
-    high = dense[...].astype(jnp.bfloat16)
-    high_ref[...] = high
-    low_ref[...] = (dense[...] - high.astype(jnp.float32)).astype(jnp.bfloat16)
-    index = lax.broadcasted_iota(jnp.int32, (nodes, nodes), 0)
-    pair_ref[...] = (index == partner_ref[...]).astype(jnp.float32).astype(jnp.bfloat16)
 
 
 def inverse_factor(gram):
@@ -86,10 +95,10 @@
 
 def iterate(
     blk_total, scale_total,
-    start_ref, degree_ref, high_ref, low_ref, pair_ref, back_ref, turned_ref, aim_ref,
+    dense_ref, back_ref, turned_ref, aim_ref, partner_ref, start_ref, scale_ref,
     subspace_ref, rayleigh_ref,
     scaled_buf, partner_buf, ahead_out, behind_out, ahead_in, behind_in,
-    turned_in, aim_in, forward_weights, *rest,
+    turned_in, aim_in, forward_weights, high_ref, low_ref, pair_ref, *rest,
 ):
     stages = group_stages(blk_total * scale_total)
     gather_bufs = rest[: len(stages)]
@@ -116,7 +125,7 @@
     for device in greeted:
         pl.semaphore_signal(barrier, inc=1, device_id=device, device_id_type=MESH)
 
-    inv_sqrt_degree = 1.0 / jnp.sqrt(degree_ref[...].astype(jnp.float32))
+    inv_sqrt_degree = scale_ref[...]
     sent = []
 
     def send(source, target, send_sem, recv_sem, device):
@@ -165,6 +174,14 @@
             pair_send.at[step], pair_recv.at[step], partner,
         )
         if step == 0:
+            for r in range(row_blocks):
+                span = slice(r * BLOCK, (r + 1) * BLOCK)
+                exact = dense_ref[span, :]
+                high = exact.astype(jnp.bfloat16)
+                high_ref[span, :] = high
+                low_ref[span, :] = (exact - high.astype(jnp.float32)).astype(jnp.bfloat16)
+                index = lax.broadcasted_iota(jnp.int32, (BLOCK, nodes), 0) + r * BLOCK
+                pair_ref[span, :] = (index == partner_ref[...]).astype(jnp.float32).astype(jnp.bfloat16)
             aim_copy.wait_recv()
         for slot in range(CROSS):
             span = slice(slot * BLOCK, (slot + 1) * BLOCK)
@@ -289,21 +306,39 @@
         vmem = pl.BlockSpec(memory_space=pltpu.VMEM)
         smem = pl.BlockSpec(memory_space=pltpu.SMEM)
         half = jnp.bfloat16
+        hbm = pl.BlockSpec(memory_space=pltpu.HBM)
+        slots = block_column.shape[0]
         prepared = pl.pallas_call(
             prepare,
             out_shape=(
-                jax.ShapeDtypeStruct((nodes, nodes), half),
-                jax.ShapeDtypeStruct((nodes, nodes), half),
-                jax.ShapeDtypeStruct((nodes, nodes), half),
+                jax.ShapeDtypeStruct((nodes, nodes), jnp.float32),
                 jax.ShapeDtypeStruct((CROSS * BLOCK, nodes), half),
                 jax.ShapeDtypeStruct((CROSS * BLOCK, BLOCK), half),
                 jax.ShapeDtypeStruct((CROSS, 2, 8, BLOCK), jnp.int32),
+                jax.ShapeDtypeStruct((1, nodes), jnp.int32),
+                jax.ShapeDtypeStruct((vectors, nodes), jnp.float32),
+                jax.ShapeDtypeStruct((1, nodes), jnp.float32),
             ),
-            in_specs=[smem, smem, smem, vmem, vmem],
-            out_specs=(vmem,) * 6,
-            scratch_shapes=[pltpu.VMEM((nodes, nodes), jnp.float32)],
+            in_specs=[smem] + [hbm] * 6,
+            out_specs=(vmem,) * 7,
+            scratch_shapes=[
+                pltpu.SMEM((slots,), jnp.int32),
+                pltpu.SMEM((slots,), jnp.int32),
+                pltpu.VMEM(blocks.shape, half),
+                pltpu.VMEM((1, nodes), jnp.int32),
+                pltpu.SemaphoreType.DMA((6,)),
+            ],
             compiler_params=pltpu.CompilerParams(vmem_limit_bytes=32 * 2**20),
-        )(block_column, block_target, block_count, blocks, partner.reshape(1, nodes))
+        )(
+            block_count,
+            *(
+                pltpu.with_memory_space_constraint(array, pltpu.HBM)
+                for array in (
+                    block_column, block_target, blocks,
+                    partner.reshape(1, nodes), start_block, degree.reshape(1, nodes),
+                )
+            ),
+        )
         steps = STEPS
         edge = pltpu.VMEM((steps, 2 * vectors, CROSS * BLOCK), half)
         counts = sum(size for _, size in stages)
@@ -313,7 +348,7 @@
                 jax.ShapeDtypeStruct((vectors, nodes), jnp.float32),
                 jax.ShapeDtypeStruct((vectors, vectors), jnp.float32),
             ),
-            in_specs=[vmem] * 8,
+            in_specs=[vmem] * 7,
             out_specs=(vmem, vmem),
             scratch_shapes=[
                 pltpu.VMEM((steps, 2 * vectors, nodes), half),
@@ -322,6 +357,9 @@
                 pltpu.VMEM((CROSS * BLOCK, BLOCK), half),
                 pltpu.VMEM((CROSS, 2, 8, BLOCK), jnp.int32),
                 pltpu.VMEM((CROSS * BLOCK, nodes), half),
+                pltpu.VMEM((nodes, nodes), half),
+                pltpu.VMEM((nodes, nodes), half),
+                pltpu.VMEM((nodes, nodes), half),
                 *[
                     pltpu.VMEM((steps, size, vectors // 2, 2 * vectors), jnp.float32)
                     for _, size in stages
@@ -336,7 +374,7 @@
             compiler_params=pltpu.CompilerParams(
                 collective_id=0, has_side_effects=True, vmem_limit_bytes=40 * 2**20
             ),
-        )(start_block, degree.reshape(1, nodes), *prepared)
+        )(*prepared)
 
     return jax.shard_map(
         shards,

time: 47.6 us -> 41.7 us (0.88)
  local copies, waits for them, and re-layouts: 6.16 us -> 1.32 us
  Pallas kernels: 39.8 us -> 39.2 us
    unnamed x14 -> x2, local copies, waits for them, and re-layouts: 6.16 us -> 1.32 us
    pallas_call x1, Pallas kernels: 37.8 us -> 36.2 us  [shards(): pl.pallas_call(functools.partial(iterate, blk_total, scale_total), out_sh...]
    pallas_call x1, Pallas kernels: 1.92 us -> 3 us  [shards(): pl.pallas_call(prepare, out_shape=(jax.ShapeDtypeStruct((nodes, nodes), j...]
where the time goes in v3:
time: 41.7 us; the launch traced here: 41.8 us
  Pallas kernels  39.2 us (94%)
  local copies, waits for them, and re-layouts  1.32 us (3%)
  between operations  1.29 us (3%)
    pallas_call x1, Pallas kernels, shards(): pl.pallas_call(functools.partial(iterate, blk_total, scale_total), out_sh...  36.2 us
    pallas_call x1, Pallas kernels, shards(): pl.pallas_call(prepare, out_shape=(jax.ShapeDtypeStruct((nodes, nodes), j...  3 us
    unnamed x2, local copies, waits for them, and re-layouts  1.32 us

profile of v3, /device:TPU:0, one launch (start us, length us, event | category | flops | bytes accessed | tf_op | source)
XLA Modules:
  0.0 41.8 jit_solution(518510412165246244)
XLA Ops:
  1.3 3.0 %shard_map.86 = (f32[1024,1024]{1,0:T(8,128)S(1)}, bf16[256,1024]{1,0:T(8,128)(2,1)S(1)}, bf16[256,128]{1,0:T(8,128)(2,1)S(1)}, s32[2,2,8,128]{3,2,1,0:T(8,128)S...) custom-call(s32[1]{0:T(128)S(6)} %copy.11.count_ref, s32[32]{0:T(128)} %column_src.1, ...), custom_call_target="tpu_custom_call" | custom-call | tf_op jit(solution)/shard_map/pallas_call | solution.py:311
  4.3 36.2 %shard_map.87 = (f32[64,1024]{1,0:T(8,128)S(1)}, f32[64,64]{1,0:T(8,128)S(1)}) custom-call(f32[1024,1024]{1,0:T(8,128)S(1)} %get-tuple-element.9.dense_ref, bf16[256,1024]{1,0:T(8,128)(2,1)S(1)} %get-tuple-element.10.back_ref, bf16[256,128]{1,0:T(8,128)(2,1)S(1)} %get-tuple-element.11.turned_ref, s32[2,2,8,128]{3,2,1,0:T(8,128)S(1)} %get-tuple-element.12.aim_ref, ...), custom_call_target="tpu_custom_call" | custom-call | tf_op jit(solution)/shard_map/pallas_call | solution.py:345
  40.5 0.7 %copy.12 = f32[64,1024]{1,0:T(8,128)} copy(f32[64,1024]{1,0:T(8,128)S(1)} %get-tuple-element.18) | data formatting | bytes 524288
  41.2 0.6 %copy.13 = f32[64,64]{1,0:T(8,128)} copy(f32[64,64]{1,0:T(8,128)S(1)} %get-tuple-element.19) | data formatting | bytes 32768
